TPU v7x, 32 devices: a whole 2x2x4 slice. The times are simulated.
32 devices in a mesh: wide: 8 (over y, x, core), narrow: 4 (over z).
Axes of the slice: x: 2, y: 2, z: 4, core: 2. Of those that a mesh axis runs over, the one named last changes fastest.
Arguments:
- state: float32 [4, 64, 64, 2048], P(None, 'narrow', None, 'wide'), may hold values from -6 to 6
- stiffness: float32 [64, 64, 2048], P('narrow', None, 'wide'), may hold values from 0.5 to 1.5
- liner_cells: int32 [4, 8, 8, 128], P('narrow', 'wide'), may hold values from 0 to 262143, as said below
- neighbour_cells: int32 [4, 8, 8, 128], P('narrow', 'wide'), may hold values from 0 to 262143, as said below
- send_counts: int32 [4, 8, 8], P('narrow', 'wide'), may hold values from 1 to 128, as said below
- history: float32 [4, 8, 8, 128, 512], P('narrow', 'wide'), may hold values from -6 to 6
- slot_panel: int32 [4, 8, 8, 128], P('narrow', 'wide'), may hold values from 0 to 3
- kernels: float32 [32, 512], P('wide'), may hold values from -0.25 to 0.25
- conductance: float32 [32], P('wide'), may hold values from 0.2 to 1
Outputs:
- state_out: float32 [4, 64, 64, 2048], P(None, 'narrow', None, 'wide')
Inputs may be any that keep to these rules, and one draw needn't show every extreme that they name: `liner_cells`: A cell of tile (j, w) in its own numbering (r * 64 + z) * 256 + t with 1 <= z <= 62; slots beyond the live count hold such cells too and carry nothing. `neighbour_cells`: the cell one axial plane beside the slot's cell, same r and t. `send_counts`: for every radial index j one owner receives exactly 128 live slots from every tile.
All inputs are finite; a program needn't handle non-finite values.
Results may differ from a plain program's by a relative error of at most 0.0003.
Values sent between devices are 32-bit elements; how exact they have to be, the bound alone decides.
A program may use at most 64 MiB of HBM per device.

v0:
```python
import functools

import jax
import jax.numpy as jnp
from jax import lax
from jax.experimental import pallas as pl
from jax.experimental.pallas import tpu as pltpu
from jax.sharding import PartitionSpec as P

ITERS = 4
WIDE_HALO = 6
THIN_HALO = 3
STEP = 0.5 / 60.0
MESH = pl.DeviceIdType.MESH
F32 = jnp.float32
BF16 = jnp.bfloat16


def split(values):
    high = values.astype(BF16)
    return high, (values - high.astype(F32)).astype(BF16)


def dot(a, b):
    return jnp.dot(a, b, preferred_element_type=F32)


def band(offset):
    value = jnp.where(jnp.abs(offset) == 1, 45.0, 0.0)
    value = jnp.where(jnp.abs(offset) == 2, -9.0, value)
    value = jnp.where(jnp.abs(offset) == 3, 1.0, value)
    return jnp.where(offset < 0, -value, value)


def iota(shape, dim):
    return lax.broadcasted_iota(jnp.int32, shape, dim)


def kernel(
    n_wide,
    n_narrow,
    state,
    stiff_in,
    cells_ref,
    beside_ref,
    counts_ref,
    history_in,
    panel_ref,
    kernels_ref,
    conduct_ref,
    out,
    stiff,
    history,
    halo,
    thin,
    edge_send,
    edge_recv,
    around_side,
    pick,
    spread,
    column,
    x_high,
    x_low,
    w_high,
    w_low,
    base,
    bands,
    blocks,
    answer_send,
    answer_recv,
    stage,
    coefs,
    walls,
    toeplitz,
    constants,
    load_sem,
    radial_send,
    radial_recv,
    thin_send,
    thin_recv,
    edge_send_sem,
    edge_recv_sem,
    answer_send_sem,
    answer_recv_sem,
):
    wide = lax.axis_index("wide")
    narrow = lax.axis_index("narrow")
    layers, planes, around = out.shape[1:]
    rows = layers * planes
    slots = panel_ref.shape[1]
    panels, taps = kernels_ref.shape
    left, right = lax.rem(wide + n_wide - 1, n_wide), lax.rem(wide + 1, n_wide)
    has_low, has_high = narrow > 0, narrow < n_narrow - 1

    loads = [
        pltpu.make_async_copy(state.at[k], out.at[k], load_sem.at[k]) for k in range(4)
    ]
    loads.append(pltpu.make_async_copy(history_in, history, load_sem.at[4]))
    loads.append(pltpu.make_async_copy(stiff_in, stiff, load_sem.at[5]))
    for which in (0, 3, 4, 1, 2, 5):
        loads[which].start()

    barrier = pltpu.get_barrier_semaphore()
    for k in range(1, n_wide):
        peer = lax.rem(wide + k, n_wide)
        pl.semaphore_signal(barrier, inc=1, device_id={"wide": peer}, device_id_type=MESH)

    @pl.when(has_low)
    def _():
        pl.semaphore_signal(
            barrier, inc=1, device_id={"narrow": narrow - 1}, device_id_type=MESH
        )

    @pl.when(has_high)
    def _():
        pl.semaphore_signal(
            barrier, inc=1, device_id={"narrow": narrow + 1}, device_id_type=MESH
        )

    @pl.when(jnp.logical_not(has_low))
    def _():
        halo[:, 0] = jnp.zeros(halo.shape[:1] + halo.shape[2:], F32)
        thin[0] = jnp.zeros(thin.shape[1:], F32)

    @pl.when(jnp.logical_not(has_high))
    def _():
        halo[:, 1] = jnp.zeros(halo.shape[:1] + halo.shape[2:], F32)
        thin[1] = jnp.zeros(thin.shape[1:], F32)

    beside = jnp.where(has_low, 1, 0) + jnp.where(has_high, 1, 0)
    pl.semaphore_wait(barrier, n_wide - 1 + beside)

    def radial_copy(source, step, side, peer=None):
        if peer is None:
            peer = narrow - 1 if side == 0 else narrow + 1
        first = 0 if side == 0 else layers - WIDE_HALO
        return pltpu.make_async_remote_copy(
            src_ref=source.at[0, pl.ds(first, WIDE_HALO)],
            dst_ref=halo.at[step, 1 - side],
            send_sem=radial_send.at[step, side],
            recv_sem=radial_recv.at[step, 1 - side],
            device_id={"narrow": peer},
            device_id_type=MESH,
        )

    def thin_copy(side, peer=None):
        if peer is None:
            peer = narrow - 1 if side == 0 else narrow + 1
        first = 0 if side == 0 else layers - THIN_HALO
        return pltpu.make_async_remote_copy(
            src_ref=state.at[1, pl.ds(first, THIN_HALO)],
            dst_ref=thin.at[1 - side],
            send_sem=thin_send.at[side],
            recv_sem=thin_recv.at[1 - side],
            device_id={"narrow": peer},
            device_id_type=MESH,
        )

    def radial_arrival(step, side):
        return radial_copy(out, step, 1 - side, narrow - 1 if side == 0 else narrow + 1)

    def thin_arrival(side):
        return thin_copy(1 - side, narrow - 1 if side == 0 else narrow + 1)

    def edge_copy(slot, side):
        return pltpu.make_async_remote_copy(
            src_ref=edge_send.at[slot, side],
            dst_ref=edge_recv.at[slot, 1 - side],
            send_sem=edge_send_sem.at[slot, side],
            recv_sem=edge_recv_sem.at[slot, 1 - side],
            device_id={"wide": left if side == 0 else right},
            device_id_type=MESH,
        )

    sides = ((0, has_low), (1, has_high))
    for side, there in sides:

        @pl.when(there)
        def _(side=side):
            radial_copy(state, 0, side).start()
            thin_copy(side).start()

    lane = iota((planes, 128), 1)

    def pack(field, slot):
        low = jnp.zeros((planes, 128), F32)
        high = jnp.zeros((planes, 128), F32)
        for r in range(layers):
            here = (lane >= 8 * r) & (lane < 8 * r + 8)
            first = out[field, r, :, 0:128]
            last = out[field, r, :, around - 128 : around]
            low = jnp.where(here, pltpu.roll(first, 8 * r, 1) if r else first, low)
            high = jnp.where(here, pltpu.roll(last, (8 * r + 8) % 128, 1), high)
        edge_send[slot, 0] = low
        edge_send[slot, 1] = high
        edge_copy(slot, 0).start()
        edge_copy(slot, 1).start()

    def unpack(slot, r):
        low = edge_recv[slot, 1]
        high = edge_recv[slot, 0]
        low = pltpu.roll(low, (128 - 8 * r) % 128, 1) if r else low
        turn = (120 - 8 * r) % 128
        high = pltpu.roll(high, turn, 1) if turn else high
        return jnp.where(lane < 8, low, jnp.where(lane >= 120, high, 0.0))

    def set_split(r):
        high, low = split(out[0, r])
        x_high[r, :, 0:around] = high
        x_low[r, :, 0:around] = low

    loads[0].wait()
    pack(0, 0)
    loads[3].wait()
    pack(3, ITERS)
    for r in range(layers):
        set_split(r)

    turned = jnp.where(iota((taps, taps), 0) + iota((taps, taps), 1) == taps - 1, 1.0, 0.0)
    backward = jnp.dot(
        kernels_ref[...], turned, precision=lax.Precision.HIGHEST, preferred_element_type=F32
    )
    toeplitz[...] = jnp.zeros_like(toeplitz)
    constants[...] = jnp.zeros_like(constants)
    late = iota((1, taps), 1)
    for q in range(panels):
        row = backward[q : q + 1]
        for lag in range(ITERS):
            shifted = pltpu.roll(row, lag, 1) if lag else row
            toeplitz[8 * q + lag : 8 * q + lag + 1] = jnp.where(late >= lag, shifted, 0.0)
        constants[8 * q + 4 : 8 * q + 5] = jnp.full((1, slots), conduct_ref[q], F32)
        for k in range(ITERS - 1):
            constants[8 * q + 5 + k : 8 * q + 6 + k] = jnp.broadcast_to(
                kernels_ref[q : q + 1, k : k + 1], (1, slots)
            )
    loads[4].wait()
    ours = iota((8 * panels, slots), 0) >> 3

    @pl.loop(0, n_wide)
    def _(o):
        full = lax.dot_general(
            toeplitz[...],
            history[pl.ds(pl.multiple_of(o * slots, slots), slots)],
            (((1,), (1,)), ((), ())),
            precision=lax.Precision.HIGHEST,
            preferred_element_type=F32,
        )
        chosen = panel_ref[pl.ds(o, 1)] == ours
        terms = jnp.where(chosen, full + constants[...], 0.0)
        answer_send[o] = jnp.sum(terms.reshape(panels, 8, slots), axis=0)

    def answer_copy(k):
        peer = lax.rem(wide + k, n_wide)
        return pltpu.make_async_remote_copy(
            src_ref=answer_send.at[peer],
            dst_ref=answer_recv.at[wide],
            send_sem=answer_send_sem.at[k],
            recv_sem=answer_recv_sem.at[k],
            device_id={"wide": peer},
            device_id_type=MESH,
        )

    for k in range(1, n_wide):
        answer_copy(k).start()
    answer_recv[wide] = answer_send[wide]

    ring = around + 128
    gap = iota((ring, ring), 0) - iota((ring, ring), 1)
    gap = jnp.where(gap > ring // 2, gap - ring, jnp.where(gap < -(ring // 2), gap + ring, gap))
    bands[...] = band(gap).astype(BF16)
    size = blocks.shape[0]
    at_row, at_col = iota((size, size), 0), iota((size, size), 1)
    blocks[...] = jnp.where(
        (at_row // planes) == (at_col // planes), band(at_col - at_row), 0.0
    ).astype(BF16)

    shift = around.bit_length() - 1
    cells = cells_ref[...]
    own_row = cells >> shift
    side_row = beside_ref[...] >> shift
    stage[...] = jnp.zeros_like(stage)
    stage[0:n_wide] = own_row.astype(F32)
    stage[n_wide : 2 * n_wide] = (cells & (around - 1)).astype(F32)
    upright = jnp.transpose(stage[...])
    place = iota((slots, rows), 1).astype(F32)
    where = iota((slots, around), 1).astype(F32)
    level = iota((rows, slots), 0)
    for o in range(n_wide):
        span = slice(o * slots, (o + 1) * slots)
        pick[span] = jnp.where(place == upright[:, o : o + 1], 1.0, 0.0).astype(BF16)
        column[span] = jnp.where(
            where == upright[:, n_wide + o : n_wide + o + 1], 1.0, 0.0
        )
        spread[:, span] = (
            jnp.where(level == own_row[o : o + 1], 3.0, 0.0)
            + jnp.where(level == side_row[o : o + 1], 2.0, 0.0)
        ).astype(BF16)

    walls[...] = jnp.zeros_like(walls)
    live = jnp.where(iota((slots, n_wide), 0) < counts_ref[...], 1.0, 0.0)

    for k in range(1, n_wide):
        answer_copy(k).wait_recv()
    for o in range(n_wide):
        for m in range(8):
            stage[m * n_wide + o : m * n_wide + o + 1] = answer_recv[o, m : m + 1]
    upright = jnp.transpose(stage[...])
    for m in range(8):
        coefs[m] = upright[:, m * n_wide : (m + 1) * n_wide]

    edge_copy(ITERS, 0).wait_recv()
    edge_copy(ITERS, 1).wait_recv()
    for r in range(layers):
        around_side[r] = unpack(ITERS, r)
    for which in (1, 2, 5):
        loads[which].wait()

    group = size // planes
    fan = 4

    def pressure_at(step, r):
        if r < 0:
            return halo[step, 0, r + WIDE_HALO]
        if r >= layers:
            return halo[step, 1, r - layers]
        return out[0, r]

    def radial_at(r):
        if r < 0:
            return thin[0, r + THIN_HALO]
        if r >= layers:
            return thin[1, r - layers]
        return out[1, r]

    def differ(get, r):
        return (
            45.0 * (get(r + 1) - get(r - 1))
            - 9.0 * (get(r + 2) - get(r - 2))
            + (get(r + 3) - get(r - 3))
        )

    @pl.loop(0, ITERS)
    def _(step):
        for first in range(0, n_wide, fan):
            span = slice(first * slots, (first + fan) * slots)
            low = pick[span]
            found = dot(low, x_high[:, :, 0:around].reshape(rows, around)) + dot(
                low, x_low[:, :, 0:around].reshape(rows, around)
            )
            wall = jnp.sum(found * column[span], axis=1, keepdims=True)
            for o in range(fan):
                walls[0, :, first + o : first + o + 1] = wall[o * slots : (o + 1) * slots]
        wall = walls[0]
        velocity = coefs[4] * wall + coefs[step]
        for k in range(1, ITERS):
            velocity = velocity + coefs[4 + k] * walls[k]
        for k in range(ITERS - 1, 0, -1):
            walls[k] = walls[k - 1]
        flux = velocity * live
        for o in range(n_wide):
            span = slice(o * slots, (o + 1) * slots)
            high, low = split(flux[:, o : o + 1] * column[span])
            w_high[span] = high
            w_low[span] = low

        edge_copy(step, 0).wait_recv()
        edge_copy(step, 1).wait_recv()
        for r in range(layers):
            high, low = split(unpack(step, r))
            x_high[r, :, around:ring] = high
            x_low[r, :, around:ring] = low

        @pl.loop(0, layers // group)
        def _(chunk):
            part = pl.ds(chunk * group, group)
            span = pl.ds(pl.multiple_of(chunk * size, size), size)

            def flat(ref, width):
                return ref.reshape(size, width)

            high, low = flat(x_high[part], ring), flat(x_low[part], ring)
            along = dot(blocks[...], high[:, :around]) + dot(blocks[...], low[:, :around])
            axial = flat(out[2, part], around) - STEP * along
            out[2, part] = axial.reshape(group, planes, around)
            turn = dot(high, bands[...]) + dot(low, bands[...])
            inner = flat(out[3, part], around) - STEP * turn[:, :around]
            outer = flat(around_side[part], 128) - STEP * turn[:, around:]
            out[3, part] = inner.reshape(group, planes, around)
            around_side[part] = outer.reshape(group, planes, 128)
            high, low = split(axial)
            total = dot(blocks[...], high) + dot(blocks[...], low)
            for block, at in ((inner, slice(0, around)), (outer, slice(around, ring))):
                high, low = split(block)
                kept = bands[at, :around]
                total = total + (dot(high, kept) + dot(low, kept))
            added = dot(spread[span], w_high[...]) + dot(spread[span], w_low[...])
            base[part] = (
                flat(out[0, part], around)
                - (STEP * flat(stiff[part], around)) * total
                - 0.1 * added
            ).reshape(group, planes, around)

        get = functools.partial(pressure_at, step)
        for r in range(THIN_HALO, layers - THIN_HALO):
            out[1, r] = out[1, r] - STEP * differ(get, r)
        for side, there in sides:

            @pl.when(there)
            def _(side=side):
                radial_arrival(step, side).wait_recv()

                @pl.when(step == 0)
                def _():
                    thin_arrival(side).wait_recv()

        for r in range(THIN_HALO):
            out[1, r] = out[1, r] - STEP * differ(get, r)
            top = layers - 1 - r
            out[1, top] = out[1, top] - STEP * differ(get, top)
        for side, there in sides:

            @pl.when(there)
            def _(side=side):
                for k in range(THIN_HALO):
                    r = k - THIN_HALO if side == 0 else layers + k
                    thin[side, k] = thin[side, k] - STEP * differ(get, r)

                radial_copy(out, step, side).wait_send()

        def renew(r):
            out[0, r] = base[r] - (STEP * stiff[r]) * differ(radial_at, r)

        for r in range(WIDE_HALO):
            renew(r)

        @pl.when((step < ITERS - 1) & has_low)
        def _():
            radial_copy(out, step + 1, 0).start()

        for r in range(layers - WIDE_HALO, layers):
            renew(r)

        @pl.when((step < ITERS - 1) & has_high)
        def _():
            radial_copy(out, step + 1, 1).start()

        for r in range(WIDE_HALO, layers - WIDE_HALO):
            renew(r)

        @pl.when(step < ITERS - 1)
        def _():
            pack(0, step + 1)
            for r in range(layers):
                set_split(r)

    for side, there in sides:

        @pl.when(there)
        def _(side=side):
            thin_copy(side).wait_send()

    for slot in range(ITERS + 1):
        edge_copy(slot, 0).wait_send()
        edge_copy(slot, 1).wait_send()
    for k in range(1, n_wide):
        answer_copy(k).wait_send()


def shards(n_wide, n_narrow, *arrays):
    (state, stiffness, cells, besides, counts, history, panel, kernels, conductance) = arrays
    _, layers, planes, around = state.shape
    peers, slots = cells.shape[2:]
    taps = kernels.shape[1]
    panels = kernels.shape[0]
    rows, count, ring = layers * planes, peers * slots, around + 128
    group = max(1, min(layers, 256 // planes))
    any_space = pl.BlockSpec(memory_space=pl.ANY)
    vmem = pl.BlockSpec(memory_space=pltpu.VMEM)
    dma = pltpu.SemaphoreType.DMA
    scratch = [
        pltpu.VMEM((layers, planes, around), F32),
        pltpu.VMEM((count, taps), F32),
        pltpu.VMEM((ITERS, 2, WIDE_HALO, planes, around), F32),
        pltpu.VMEM((2, THIN_HALO, planes, around), F32),
        pltpu.VMEM((ITERS + 1, 2, planes, 128), F32),
        pltpu.VMEM((ITERS + 1, 2, planes, 128), F32),
        pltpu.VMEM((layers, planes, 128), F32),
        pltpu.VMEM((count, rows), BF16),
        pltpu.VMEM((rows, count), BF16),
        pltpu.VMEM((count, around), F32),
        pltpu.VMEM((layers, planes, ring), BF16),
        pltpu.VMEM((layers, planes, ring), BF16),
        pltpu.VMEM((count, around), BF16),
        pltpu.VMEM((count, around), BF16),
        pltpu.VMEM((layers, planes, around), F32),
        pltpu.VMEM((ring, ring), BF16),
        pltpu.VMEM((group * planes, group * planes), BF16),
        pltpu.VMEM((peers, 8, slots), F32),
        pltpu.VMEM((peers, 8, slots), F32),
        pltpu.VMEM((max(128, 8 * peers), slots), F32),
        pltpu.VMEM((8, slots, peers), F32),
        pltpu.VMEM((ITERS, slots, peers), F32),
        pltpu.VMEM((8 * panels, taps), F32),
        pltpu.VMEM((8 * panels, slots), F32),
        dma((6,)),
        dma((ITERS, 2)),
        dma((ITERS, 2)),
        dma((2,)),
        dma((2,)),
        dma((ITERS + 1, 2)),
        dma((ITERS + 1, 2)),
        dma((peers,)),
        dma((peers,)),
    ]
    return pl.pallas_call(
        functools.partial(kernel, n_wide, n_narrow),
        out_shape=jax.ShapeDtypeStruct(state.shape, F32),
        in_specs=[any_space, any_space, vmem, vmem, vmem, any_space, vmem, vmem]
        + [pl.BlockSpec(memory_space=pltpu.SMEM)],
        out_specs=vmem,
        scratch_shapes=scratch,
        compiler_params=pltpu.CompilerParams(
            collective_id=0, has_side_effects=True, vmem_limit_bytes=56 * 1024 * 1024
        ),
    )(
        state,
        stiffness,
        cells.reshape(peers, slots),
        besides.reshape(peers, slots),
        counts.reshape(1, peers),
        history.reshape(count, taps),
        panel.reshape(peers, slots),
        kernels,
        conductance,
    )


def solution(mesh):
    return jax.shard_map(
        functools.partial(shards, mesh.shape["wide"], mesh.shape["narrow"]),
        mesh=mesh,
        in_specs=(
            P(None, "narrow", None, "wide"),
            P("narrow", None, "wide"),
            P("narrow", "wide", None, None),
            P("narrow", "wide", None, None),
            P("narrow", "wide", None),
            P("narrow", "wide", None, None, None),
            P("narrow", "wide", None, None),
            P("wide", None),
            P("wide"),
        ),
        out_specs=P(None, "narrow", None, "wide"),
        check_vma=False,
    )
```

profile of v0, /device:TPU:0, one launch (start us, length us, event | category | flops | bytes accessed | tf_op | source)
XLA Modules:
  0.0 58.4 jit_solution(3228340289168658758)
XLA Ops:
  0.0 53.7 %shard_map.91 = f32[4,16,64,256]{3,2,1,0:T(8,128)} custom-call(f32[4,16,64,256]{3,2,1,0:T(8,128)} %state.1, f32[16,64,256]{2,1,0:T(8,128)} %stiff_in.1, s32[8,128]{1,0:T(8,128)} %bitcast.6, s32[8,128]{1,0:T(8,128)} %bitcast.7, s32[1,8]{1,0:T(1,128)} %bitcast.9, f32[1024,512]{1,0:T(8,128)} %bitcast.5, s32[8,128]{1,0:T(8,128)} %bitcast.8, ...), custom_call_target="tpu_custom_call" | custom-call | tf_op jit(solution)/shard_map/pallas_call | solution.py:515
  53.7 4.7 %copy.11 = f32[4,16,64,256]{3,2,1,0:T(8,128)} copy(f32[4,16,64,256]{3,2,1,0:T(8,128)} %shard_map.91) | data formatting | bytes 8388608
where the time goes:
time: 58.6 us; the launch traced here: 58.4 us
  Pallas kernels  53.7 us (92%)
  local copies, waits for them, and re-layouts  4.7 us (8%)
    pallas_call x1, Pallas kernels, shards(): pl.pallas_call(functools.partial(kernel, n_wide, n_narrow), out_shape=jax...  53.7 us
    unnamed x1, local copies, waits for them, and re-layouts  4.7 us

commit v1 on v0

--- a/solution.py
+++ b/solution.py
@@ -41,14 +41,19 @@
     n_narrow,
     state,
     stiff_in,
+    cells_in,
+    beside_in,
+    counts_in,
+    history_in,
+    panel_in,
+    kernels_in,
+    conduct_ref,
+    out,
     cells_ref,
     beside_ref,
     counts_ref,
-    history_in,
     panel_ref,
     kernels_ref,
-    conduct_ref,
-    out,
     stiff,
     history,
     halo,
@@ -87,8 +92,8 @@
     narrow = lax.axis_index("narrow")
     layers, planes, around = out.shape[1:]
     rows = layers * planes
-    slots = panel_ref.shape[1]
-    panels, taps = kernels_ref.shape
+    slots = panel_in.shape[1]
+    panels, taps = kernels_in.shape
     left, right = lax.rem(wide + n_wide - 1, n_wide), lax.rem(wide + 1, n_wide)
     has_low, has_high = narrow > 0, narrow < n_narrow - 1
 
@@ -97,7 +102,16 @@
     ]
     loads.append(pltpu.make_async_copy(history_in, history, load_sem.at[4]))
     loads.append(pltpu.make_async_copy(stiff_in, stiff, load_sem.at[5]))
-    for which in (0, 3, 4, 1, 2, 5):
+    small = (
+        (cells_in, cells_ref),
+        (beside_in, beside_ref),
+        (counts_in, counts_ref),
+        (panel_in, panel_ref),
+        (kernels_in, kernels_ref),
+    )
+    for k, (source, target) in enumerate(small):
+        loads.append(pltpu.make_async_copy(source, target, load_sem.at[6 + k]))
+    for which in (6, 7, 8, 9, 10, 0, 4, 3, 1, 2, 5):
         loads[which].start()
 
     barrier = pltpu.get_barrier_semaphore()
@@ -209,17 +223,14 @@
         x_high[r, :, 0:around] = high
         x_low[r, :, 0:around] = low
 
-    loads[0].wait()
-    pack(0, 0)
-    loads[3].wait()
-    pack(3, ITERS)
-    for r in range(layers):
-        set_split(r)
-
-    turned = jnp.where(iota((taps, taps), 0) + iota((taps, taps), 1) == taps - 1, 1.0, 0.0)
-    backward = jnp.dot(
-        kernels_ref[...], turned, precision=lax.Precision.HIGHEST, preferred_element_type=F32
-    )
+    for which in range(6, 11):
+        loads[which].wait()
+    turned = jnp.where(
+        iota((taps, taps), 0) + iota((taps, taps), 1) == taps - 1, 1.0, 0.0
+    ).astype(BF16)
+    high, low = split(kernels_ref[...])
+    rest = (kernels_ref[...] - high.astype(F32) - low.astype(F32)).astype(BF16)
+    backward = dot(high, turned) + dot(low, turned) + dot(rest, turned)
     toeplitz[...] = jnp.zeros_like(toeplitz)
     constants[...] = jnp.zeros_like(constants)
     late = iota((1, taps), 1)
@@ -236,18 +247,26 @@
     loads[4].wait()
     ours = iota((8 * panels, slots), 0) >> 3
 
-    @pl.loop(0, n_wide)
-    def _(o):
-        full = lax.dot_general(
-            toeplitz[...],
-            history[pl.ds(pl.multiple_of(o * slots, slots), slots)],
-            (((1,), (1,)), ((), ())),
-            precision=lax.Precision.HIGHEST,
-            preferred_element_type=F32,
-        )
-        chosen = panel_ref[pl.ds(o, 1)] == ours
-        terms = jnp.where(chosen, full + constants[...], 0.0)
-        answer_send[o] = jnp.sum(terms.reshape(panels, 8, slots), axis=0)
+    lead, tail = split(toeplitz[...])
+    both = jnp.concatenate([lead, tail], axis=0)
+
+    def against(a, b):
+        return lax.dot_general(a, b, (((1,), (1,)), ((), ())), preferred_element_type=F32)
+
+    pairs = 2
+
+    @pl.loop(0, n_wide // pairs)
+    def _(block):
+        size = pairs * slots
+        high, low = split(history[pl.ds(pl.multiple_of(block * size, size), size)])
+        full = against(both, high)
+        full = full[: 8 * panels] + (full[8 * panels :] + against(lead, low))
+        for k in range(pairs):
+            o = block * pairs + k
+            chosen = panel_ref[pl.ds(o, 1)] == ours
+            terms = full[:, k * slots : (k + 1) * slots] + constants[...]
+            terms = jnp.where(chosen, terms, 0.0)
+            answer_send[o] = jnp.sum(terms.reshape(panels, 8, slots), axis=0)
 
     def answer_copy(k):
         peer = lax.rem(wide + k, n_wide)
@@ -263,6 +282,12 @@
     for k in range(1, n_wide):
         answer_copy(k).start()
     answer_recv[wide] = answer_send[wide]
+    loads[0].wait()
+    pack(0, 0)
+    loads[3].wait()
+    pack(3, ITERS)
+    for r in range(layers):
+        set_split(r)
 
     ring = around + 128
     gap = iota((ring, ring), 0) - iota((ring, ring), 1)
@@ -474,10 +499,15 @@
     panels = kernels.shape[0]
     rows, count, ring = layers * planes, peers * slots, around + 128
     group = max(1, min(layers, 256 // planes))
-    any_space = pl.BlockSpec(memory_space=pl.ANY)
+    any_space = pl.BlockSpec(memory_space=pltpu.HBM)
     vmem = pl.BlockSpec(memory_space=pltpu.VMEM)
     dma = pltpu.SemaphoreType.DMA
     scratch = [
+        pltpu.VMEM((peers, slots), jnp.int32),
+        pltpu.VMEM((peers, slots), jnp.int32),
+        pltpu.VMEM((1, peers), jnp.int32),
+        pltpu.VMEM((peers, slots), jnp.int32),
+        pltpu.VMEM((panels, taps), F32),
         pltpu.VMEM((layers, planes, around), F32),
         pltpu.VMEM((count, taps), F32),
         pltpu.VMEM((ITERS, 2, WIDE_HALO, planes, around), F32),
@@ -502,7 +532,7 @@
         pltpu.VMEM((ITERS, slots, peers), F32),
         pltpu.VMEM((8 * panels, taps), F32),
         pltpu.VMEM((8 * panels, slots), F32),
-        dma((6,)),
+        dma((11,)),
         dma((ITERS, 2)),
         dma((ITERS, 2)),
         dma((2,)),
@@ -515,22 +545,26 @@
     return pl.pallas_call(
         functools.partial(kernel, n_wide, n_narrow),
         out_shape=jax.ShapeDtypeStruct(state.shape, F32),
-        in_specs=[any_space, any_space, vmem, vmem, vmem, any_space, vmem, vmem]
-        + [pl.BlockSpec(memory_space=pltpu.SMEM)],
+        in_specs=[any_space] * 8 + [pl.BlockSpec(memory_space=pltpu.SMEM)],
         out_specs=vmem,
         scratch_shapes=scratch,
         compiler_params=pltpu.CompilerParams(
-            collective_id=0, has_side_effects=True, vmem_limit_bytes=56 * 1024 * 1024
+            collective_id=0, has_side_effects=True, vmem_limit_bytes=32 * 1024 * 1024
         ),
     )(
-        state,
-        stiffness,
-        cells.reshape(peers, slots),
-        besides.reshape(peers, slots),
-        counts.reshape(1, peers),
-        history.reshape(count, taps),
-        panel.reshape(peers, slots),
-        kernels,
+        *[
+            pltpu.with_memory_space_constraint(array, pltpu.HBM)
+            for array in (
+                state,
+                stiffness,
+                cells.reshape(peers, slots),
+                besides.reshape(peers, slots),
+                counts.reshape(1, peers),
+                history.reshape(count, taps),
+                panel.reshape(peers, slots),
+                kernels,
+            )
+        ],
         conductance,
     )
 

time: 58.6 us -> 54.7 us (0.933)
  local copies, waits for them, and re-layouts: 4.7 us -> 2.67 us
  Pallas kernels: 53.7 us -> 51.9 us
    unnamed x1 -> x3, local copies, waits for them, and re-layouts: 4.7 us -> 2.67 us
    pallas_call x1, Pallas kernels: 53.7 us -> 51.9 us  [shards(): pl.pallas_call(functools.partial(kernel, n_wide, n_narrow), out_shape=jax...]
where the time goes in v1:
time: 54.7 us; the launch traced here: 54.6 us
  Pallas kernels  51.9 us (95%)
  local copies, waits for them, and re-layouts  2.67 us (5%)
    pallas_call x1, Pallas kernels, shards(): pl.pallas_call(functools.partial(kernel, n_wide, n_narrow), out_shape=jax...  51.9 us
    unnamed x3, local copies, waits for them, and re-layouts  2.67 us

profile of v1, /device:TPU:0, one launch (start us, length us, event | category | flops | bytes accessed | tf_op | source)
XLA Modules:
  0.0 54.6 jit_solution(11287270195725090441)
XLA Ops:
  0.0 0.0 copy-start
  0.0 0.7 %copy-done = f32[4]{0:T(128)S(1)} copy-done((f32[4]{0:T(128)S(1)}, f32[4]{0:T(128)}, u32[]{:S(2)}) %copy-start) | copy-done | bytes 40
  0.7 51.9 %shard_map.91 = f32[4,16,64,256]{3,2,1,0:T(8,128)S(1)} custom-call(f32[4,16,64,256]{3,2,1,0:T(8,128)} %state.1, f32[16,64,256]{2,1,0:T(8,128)} %stiff_in.1, s32[8,128]{1,0:T(8,128)} %bitcast.6, s32[8,128]{1,0:T(8,128)} %bitcast.7, s32[1,8]{1,0:T(1,128)} %bitcast.9, f32[1024,512]{1,0:T(8,128)} %bitcast.5, s32[8,128]{1,0:T(8,128)} %bitcast.8, ...), custom_call_target="tpu_custom_call" | custom-call | tf_op jit(solution)/shard_map/pallas_call | solution.py:545
  52.6 2.0 %copy.11 = f32[4,16,64,256]{3,2,1,0:T(8,128)} copy(f32[4,16,64,256]{3,2,1,0:T(8,128)S(1)} %shard_map.91) | data formatting | bytes 8388608
Async XLA Ops:
  0.0 0.7 %copy-start = (f32[4]{0:T(128)S(1)}, f32[4]{0:T(128)}, u32[]{:S(2)}) copy-start(f32[4]{0:T(128)} %conduct_ref.1) | copy-start | bytes 52

commit v2 on v1

--- a/solution.py
+++ b/solution.py
@@ -91,7 +91,7 @@
     wide = lax.axis_index("wide")
     narrow = lax.axis_index("narrow")
     layers, planes, around = out.shape[1:]
-    rows = layers * planes
+    rows, middle = layers * planes, planes // 2
     slots = panel_in.shape[1]
     panels, taps = kernels_in.shape
     left, right = lax.rem(wide + n_wide - 1, n_wide), lax.rem(wide + 1, n_wide)
@@ -144,15 +144,15 @@
     beside = jnp.where(has_low, 1, 0) + jnp.where(has_high, 1, 0)
     pl.semaphore_wait(barrier, n_wide - 1 + beside)
 
-    def radial_copy(source, step, side, peer=None):
+    def radial_copy(source, step, side, half, peer=None):
         if peer is None:
             peer = narrow - 1 if side == 0 else narrow + 1
         first = 0 if side == 0 else layers - WIDE_HALO
         return pltpu.make_async_remote_copy(
-            src_ref=source.at[0, pl.ds(first, WIDE_HALO)],
-            dst_ref=halo.at[step, 1 - side],
-            send_sem=radial_send.at[step, side],
-            recv_sem=radial_recv.at[step, 1 - side],
+            src_ref=source.at[0, pl.ds(first, WIDE_HALO), pl.ds(half * middle, middle)],
+            dst_ref=halo.at[step, 1 - side, :, pl.ds(half * middle, middle)],
+            send_sem=radial_send.at[step, side, half],
+            recv_sem=radial_recv.at[step, 1 - side, half],
             device_id={"narrow": peer},
             device_id_type=MESH,
         )
@@ -170,8 +170,8 @@
             device_id_type=MESH,
         )
 
-    def radial_arrival(step, side):
-        return radial_copy(out, step, 1 - side, narrow - 1 if side == 0 else narrow + 1)
+    def radial_arrival(step, side, half):
+        return radial_copy(out, step, 1 - side, half, narrow - 1 if side == 0 else narrow + 1)
 
     def thin_arrival(side):
         return thin_copy(1 - side, narrow - 1 if side == 0 else narrow + 1)
@@ -191,8 +191,9 @@
 
         @pl.when(there)
         def _(side=side):
-            radial_copy(state, 0, side).start()
+            radial_copy(state, 0, side, 0).start()
             thin_copy(side).start()
+            radial_copy(state, 0, side, 1).start()
 
     lane = iota((planes, 128), 1)
 
@@ -343,26 +344,60 @@
     group = size // planes
     fan = 4
 
-    def pressure_at(step, r):
+    def pressure_at(step, span, r):
         if r < 0:
-            return halo[step, 0, r + WIDE_HALO]
+            return halo[step, 0, r + WIDE_HALO, span]
         if r >= layers:
-            return halo[step, 1, r - layers]
-        return out[0, r]
-
-    def radial_at(r):
+            return halo[step, 1, r - layers, span]
+        return out[0, r, span]
+
+    def radial_at(span, r):
         if r < 0:
-            return thin[0, r + THIN_HALO]
+            return thin[0, r + THIN_HALO, span]
         if r >= layers:
-            return thin[1, r - layers]
-        return out[1, r]
-
-    def differ(get, r):
-        return (
-            45.0 * (get(r + 1) - get(r - 1))
-            - 9.0 * (get(r + 2) - get(r - 2))
-            + (get(r + 3) - get(r - 3))
-        )
+            return thin[1, r - layers, span]
+        return out[1, r, span]
+
+    def set_radial(span, r, values):
+        if r < 0:
+            thin[0, r + THIN_HALO, span] = values
+        elif r >= layers:
+            thin[1, r - layers, span] = values
+        else:
+            out[1, r, span] = values
+
+    def differences(get, first, last):
+        held = {r: get(r) for r in range(first - 3, last + 3)}
+        return {
+            r: (45.0 * STEP) * (held[r + 1] - held[r - 1])
+            - (9.0 * STEP) * (held[r + 2] - held[r - 2])
+            + STEP * (held[r + 3] - held[r - 3])
+            for r in range(first, last)
+        }
+
+    def sweep(half):
+        first, last = (0, planes) if half is None else (half * middle, (half + 1) * middle)
+        return lambda body: pl.loop(first // 16, last // 16)(
+            lambda k: body(pl.ds(pl.multiple_of(k * 16, 16), 16))
+        )
+
+    def push_radial(step, first, last, half=None):
+        @sweep(half)
+        def _(span):
+            slopes = differences(functools.partial(pressure_at, step, span), first, last)
+            for r, slope in slopes.items():
+                set_radial(span, r, radial_at(span, r) - slope)
+
+    def renew(first, last, half=None):
+        @sweep(half)
+        def _(span):
+            slopes = differences(functools.partial(radial_at, span), first, last)
+            for r, slope in slopes.items():
+                fresh = base[r, span] - stiff[r, span] * slope
+                out[0, r, span] = fresh
+                high, low = split(fresh)
+                x_high[r, span, 0:around] = high
+                x_low[r, span, 0:around] = low
 
     @pl.loop(0, ITERS)
     def _(step):
@@ -388,6 +423,7 @@
             w_high[span] = high
             w_low[span] = low
 
+        push_radial(step, THIN_HALO, layers - THIN_HALO)
         edge_copy(step, 0).wait_recv()
         edge_copy(step, 1).wait_recv()
         for r in range(layers):
@@ -407,7 +443,8 @@
             along = dot(blocks[...], high[:, :around]) + dot(blocks[...], low[:, :around])
             axial = flat(out[2, part], around) - STEP * along
             out[2, part] = axial.reshape(group, planes, around)
-            turn = dot(high, bands[...]) + dot(low, bands[...])
+            turn = dot(jnp.concatenate([high, low], axis=0), bands[...])
+            turn = turn[:size] + turn[size:]
             inner = flat(out[3, part], around) - STEP * turn[:, :around]
             outer = flat(around_side[part], 128) - STEP * turn[:, around:]
             out[3, part] = inner.reshape(group, planes, around)
@@ -417,66 +454,53 @@
             for block, at in ((inner, slice(0, around)), (outer, slice(around, ring))):
                 high, low = split(block)
                 kept = bands[at, :around]
-                total = total + (dot(high, kept) + dot(low, kept))
+                both = dot(jnp.concatenate([high, low], axis=0), kept)
+                total = total + (both[:size] + both[size:])
             added = dot(spread[span], w_high[...]) + dot(spread[span], w_low[...])
             base[part] = (
                 flat(out[0, part], around)
-                - (STEP * flat(stiff[part], around)) * total
+                - STEP * flat(stiff[part], around) * total
                 - 0.1 * added
             ).reshape(group, planes, around)
 
-        get = functools.partial(pressure_at, step)
-        for r in range(THIN_HALO, layers - THIN_HALO):
-            out[1, r] = out[1, r] - STEP * differ(get, r)
-        for side, there in sides:
-
-            @pl.when(there)
-            def _(side=side):
-                radial_arrival(step, side).wait_recv()
-
-                @pl.when(step == 0)
-                def _():
-                    thin_arrival(side).wait_recv()
-
-        for r in range(THIN_HALO):
-            out[1, r] = out[1, r] - STEP * differ(get, r)
-            top = layers - 1 - r
-            out[1, top] = out[1, top] - STEP * differ(get, top)
-        for side, there in sides:
-
-            @pl.when(there)
-            def _(side=side):
-                for k in range(THIN_HALO):
-                    r = k - THIN_HALO if side == 0 else layers + k
-                    thin[side, k] = thin[side, k] - STEP * differ(get, r)
-
-                radial_copy(out, step, side).wait_send()
-
-        def renew(r):
-            out[0, r] = base[r] - (STEP * stiff[r]) * differ(radial_at, r)
-
-        for r in range(WIDE_HALO):
-            renew(r)
-
-        @pl.when((step < ITERS - 1) & has_low)
-        def _():
-            radial_copy(out, step + 1, 0).start()
-
-        for r in range(layers - WIDE_HALO, layers):
-            renew(r)
-
-        @pl.when((step < ITERS - 1) & has_high)
-        def _():
-            radial_copy(out, step + 1, 1).start()
-
-        for r in range(WIDE_HALO, layers - WIDE_HALO):
-            renew(r)
+        for half in range(2):
+            for side, there in sides:
+                inside, end = (0, THIN_HALO) if side == 0 else (layers - THIN_HALO, layers)
+
+                @pl.when(there)
+                def _(side=side, half=half):
+                    radial_arrival(step, side, half).wait_recv()
+                    if half == 0:
+
+                        @pl.when(step == 0)
+                        def _():
+                            thin_arrival(side).wait_recv()
+
+                    if side == 0:
+                        push_radial(step, -THIN_HALO, THIN_HALO, half)
+                    else:
+                        push_radial(step, layers - THIN_HALO, layers + THIN_HALO, half)
+                    radial_copy(out, step, side, half).wait_send()
+
+                @pl.when(jnp.logical_not(there))
+                def _(inside=inside, end=end, half=half):
+                    push_radial(step, inside, end, half)
+
+            for side, there in sides:
+                if side == 0:
+                    renew(0, WIDE_HALO, half)
+                else:
+                    renew(layers - WIDE_HALO, layers, half)
+
+                @pl.when((step < ITERS - 1) & there)
+                def _(side=side, half=half):
+                    radial_copy(out, step + 1, side, half).start()
+
+        renew(WIDE_HALO, layers - WIDE_HALO)
 
         @pl.when(step < ITERS - 1)
         def _():
             pack(0, step + 1)
-            for r in range(layers):
-                set_split(r)
 
     for side, there in sides:
 
@@ -533,8 +557,8 @@
         pltpu.VMEM((8 * panels, taps), F32),
         pltpu.VMEM((8 * panels, slots), F32),
         dma((11,)),
-        dma((ITERS, 2)),
-        dma((ITERS, 2)),
+        dma((ITERS, 2, 2)),
+        dma((ITERS, 2, 2)),
         dma((2,)),
         dma((2,)),
         dma((ITERS + 1, 2)),

time: 54.7 us -> 51.4 us (0.940)
  Pallas kernels: 51.9 us -> 48.5 us
    pallas_call x1, Pallas kernels: 51.9 us -> 48.5 us  [shards(): pl.pallas_call(functools.partial(kernel, n_wide, n_narrow), out_shape=jax...]
where the time goes in v2:
time: 51.4 us; the launch traced here: 51.2 us
  Pallas kernels  48.5 us (94%)
  local copies, waits for them, and re-layouts  2.67 us (5%)
    pallas_call x1, Pallas kernels, shards(): pl.pallas_call(functools.partial(kernel, n_wide, n_narrow), out_shape=jax...  48.5 us
    unnamed x3, local copies, waits for them, and re-layouts  2.67 us

profile of v2, /device:TPU:0, one launch (start us, length us, event | category | flops | bytes accessed | tf_op | source)
XLA Modules:
  0.0 51.2 jit_solution(16983140156924203186)
XLA Ops:
  0.0 0.0 copy-start
  0.0 0.7 %copy-done = f32[4]{0:T(128)S(1)} copy-done((f32[4]{0:T(128)S(1)}, f32[4]{0:T(128)}, u32[]{:S(2)}) %copy-start) | copy-done | bytes 40
  0.7 48.5 %shard_map.91 = f32[4,16,64,256]{3,2,1,0:T(8,128)S(1)} custom-call(f32[4,16,64,256]{3,2,1,0:T(8,128)} %state.1, f32[16,64,256]{2,1,0:T(8,128)} %stiff_in.1, s32[8,128]{1,0:T(8,128)} %bitcast.6, s32[8,128]{1,0:T(8,128)} %bitcast.7, s32[1,8]{1,0:T(1,128)} %bitcast.9, f32[1024,512]{1,0:T(8,128)} %bitcast.5, s32[8,128]{1,0:T(8,128)} %bitcast.8, ...), custom_call_target="tpu_custom_call" | custom-call | tf_op jit(solution)/shard_map/pallas_call | solution.py:569
  49.2 2.0 %copy.11 = f32[4,16,64,256]{3,2,1,0:T(8,128)} copy(f32[4,16,64,256]{3,2,1,0:T(8,128)S(1)} %shard_map.91) | data formatting | bytes 8388608
Async XLA Ops:
  0.0 0.7 %copy-start = (f32[4]{0:T(128)S(1)}, f32[4]{0:T(128)}, u32[]{:S(2)}) copy-start(f32[4]{0:T(128)} %conduct_ref.1) | copy-start | bytes 52
